TPU v7x, 256 devices: a whole 4x4x8 slice. The times are simulated.
256 devices in a mesh: dp: 16 (over y, x), ctx: 16 (over z, core).
Axes of the slice: x: 4, y: 4, z: 8, core: 2. Of those that a mesh axis runs over, the one named last changes fastest.
Arguments:
- hidden_in: bfloat16 [16, 3072, 16384], P('dp', 'ctx'), may hold values from -8 to 8
- queries: bfloat16 [16, 3072, 1024], P('dp', 'ctx'), may hold values from -14 to 14
- grad_out: bfloat16 [16, 3072, 1024], P('dp', 'ctx'), may hold values from -6 to 6
- w_key: bfloat16 [16384, 128], P('dp'), may hold values from -1 to 1
- w_value: bfloat16 [16384, 128], P('dp'), may hold values from -0.046875 to 0.046875
- stretch_order: int32 [32], replicated, may hold values from 0 to 31, each once
- doc_lengths: int32 [16, 8], P('dp'), may hold values from 1 to 1536, 3072 in all within a row
Outputs:
- query_grad: bfloat16 [16, 3072, 1024], P('dp', 'ctx')
- key_weight_grad: float32 [16384, 128], P('dp')
- value_weight_grad: float32 [16384, 128], P('dp')
Inputs may be any that keep to these rules, and one draw needn't show every extreme that they name: `stretch_order`: every block number appears exactly once. `doc_lengths`: each sequence's lengths sum to 3072, and one of them is 1536.
All inputs are finite; a program needn't handle non-finite values.
Results may differ from a plain program's by a relative error of at most 0.03.
Values may be sent and summed in bfloat16 or wider, within the bound.
A program may use at most 128 MiB of HBM per device.

v0:
```python
import math
import jax
import jax.numpy as jnp
from jax import lax
from jax.sharding import PartitionSpec as P


def table_lookup(slots, table):
    choices_all = jnp.arange(table.shape[0], dtype=jnp.int32)
    return jnp.sum(jnp.where(slots[:, None] == choices_all[None, :], table[None, :], 0), axis=1)


def place_and_doc(stored, stretch_order, stretch_rows, doc_ends):
    place = (
        table_lookup(stored // stretch_rows, stretch_order) * stretch_rows + stored % stretch_rows
    )
    documents = jnp.sum((place[:, None] >= doc_ends[None, :]).astype(jnp.int32), axis=1)
    return (place, documents)


def attention_grads(query_rows, key_rows, value_rows, cotangent, allowed, head_count, head_dim):
    row_count = query_rows.shape[0]
    score_scale = 1.0 / math.sqrt(head_dim)
    query_heads = jnp.transpose(query_rows.reshape(row_count, head_count, head_dim), (1, 0, 2))
    cot_heads = jnp.transpose(cotangent.reshape(row_count, head_count, head_dim), (1, 0, 2))

    def one_head(running, items):
        query_one, cot_one = items
        scores = (
            jnp.dot(query_one, jnp.transpose(key_rows), preferred_element_type=jnp.float32)
            * score_scale
        )
        masked = jnp.where(allowed, scores, -jnp.inf)
        row_max = jnp.max(masked, axis=-1, keepdims=True)
        expsum = jnp.where(allowed, jnp.exp(masked - row_max), 0.0)
        probabilities = expsum / jnp.sum(expsum, axis=-1, keepdims=True)
        probs_low = probabilities.astype(jnp.bfloat16)
        attended = jnp.dot(probs_low, value_rows, preferred_element_type=jnp.float32)
        delta_rows = jnp.sum(cot_one.astype(jnp.float32) * attended, axis=-1)
        dprob = jnp.dot(cot_one, jnp.transpose(value_rows), preferred_element_type=jnp.float32)
        dscore = (probabilities * (dprob - delta_rows[:, None])).astype(jnp.bfloat16)
        query_grad = (
            jnp.dot(dscore, key_rows, preferred_element_type=jnp.float32) * score_scale
        ).astype(jnp.bfloat16)
        key_grad = (
            lax.dot_general(
                dscore, query_one, (((0,), (0,)), ((), ())), preferred_element_type=jnp.float32
            )
            * score_scale
        )
        value_grad = lax.dot_general(
            probs_low, cot_one, (((0,), (0,)), ((), ())), preferred_element_type=jnp.float32
        )
        return (running + jnp.concatenate([key_grad, value_grad], axis=1), query_grad)

    start_sum = jnp.zeros((key_rows.shape[0], 2 * head_dim), jnp.float32)
    kv_grads, query_grad = lax.scan(one_head, start_sum, (query_heads, cot_heads))
    return (
        jnp.transpose(query_grad, (1, 0, 2)).reshape(row_count, head_count * head_dim),
        kv_grads,
    )


def on_device(hidden_in, queries, grad_out, w_key, w_value, stretch_order, doc_lengths):
    inputs = hidden_in[0]
    row_count = inputs.shape[0]
    stretch_rows = row_count // 2
    head_dim = w_key.shape[1]
    head_count = queries.shape[2] // head_dim
    ctx_count = lax.axis_size("ctx")
    seq_rows = row_count * ctx_count
    stacked = jnp.concatenate([w_key, w_value], axis=1)
    columns = inputs
    projected = jnp.dot(
        columns,
        lax.all_gather(stacked, "dp", axis=0, tiled=True),
        preferred_element_type=jnp.float32,
    ).astype(jnp.bfloat16)
    gathered = lax.all_gather(projected, "ctx", axis=0, tiled=True)
    doc_ends = jnp.cumsum(doc_lengths[0])
    every_row = jnp.arange(seq_rows, dtype=jnp.int32)
    own_rows = lax.axis_index("ctx") * row_count + jnp.arange(row_count, dtype=jnp.int32)
    key_place, key_docs = place_and_doc(every_row, stretch_order, stretch_rows, doc_ends)
    query_place, query_docs = place_and_doc(own_rows, stretch_order, stretch_rows, doc_ends)
    allowed = (key_place[None, :] <= query_place[:, None]) & (
        key_docs[None, :] == query_docs[:, None]
    )
    query_grad, kv_partial = attention_grads(
        queries[0],
        gathered[:, :head_dim],
        gathered[:, head_dim:],
        grad_out[0],
        allowed,
        head_count,
        head_dim,
    )
    kv_grads = lax.psum_scatter(
        kv_partial.astype(jnp.bfloat16), "ctx", scatter_dimension=0, tiled=True
    )
    columns = inputs
    partial_rows = lax.psum_scatter(
        lax.dot_general(
            columns, kv_grads, (((0,), (0,)), ((), ())), preferred_element_type=jnp.float32
        ).astype(jnp.bfloat16),
        "dp",
        scatter_dimension=0,
        tiled=True,
    )
    weight_grads = lax.psum(partial_rows, "ctx").astype(jnp.float32)
    return (
        query_grad.reshape(1, row_count, head_count * head_dim),
        weight_grads[:, :head_dim],
        weight_grads[:, head_dim:],
    )


def solution(mesh):
    return jax.shard_map(
        on_device,
        mesh=mesh,
        in_specs=(
            P("dp", "ctx", None),
            P("dp", "ctx", None),
            P("dp", "ctx", None),
            P("dp", None),
            P("dp", None),
            P(),
            P("dp", None),
        ),
        out_specs=(P("dp", "ctx", None), P("dp", None), P("dp", None)),
        check_vma=False,
    )
```

profile of v0, /device:TPU:1, one launch (start us, length us, event | category | flops | bytes accessed | tf_op | source)
XLA Modules:
  0.0 494.5 jit_solution(5097747195582043551)
XLA Ops:
  7.2 1.9 pad_maximum_fusion
  9.2 81.4 %all-gather.3.cloned.1.call-done = bf16[16384,256]{1,0:T(8,128)(2,1)} async-done(((bf16[1024,256]{1,0:T(8,128)(2,1)}), bf16[16384,256]{1,0:T(8,128)(2,1)}) %all-gather.3.cloned.1.call-update) | async-done | bytes 8388624 | tf_op jit(solution)/shard_map/all_gather | solution.py:76
  90.6 7.6 %fusion.33 = bf16[192,256]{1,0:T(8,128)(2,1)} fusion(bf16[16384,256]{1,0:T(8,128)(2,1)} %all-gather.3.cloned.1.call-done, bf16[1,192,16384]{2,1,0:T(8,128)(2,1)} %param.9), kind=kOutput, calls=%fused_computation.39 | convolution fusion | flops 1610661888 | bytes 14778368 | tf_op jit(solution)/shard_map/dot_general | solution.py:74
  101.2 1.3 convert_reduce_fusion.1
  103.3 1.3 convert_reduce_fusion
  104.6 33.1 %all-gather.5.cloned.1.call-done = bf16[3072,256]{1,0:T(8,128)(2,1)} async-done(((bf16[192,256]{1,0:T(8,128)(2,1)}), bf16[3072,256]{1,0:T(8,128)(2,1)}) %all-gather.5.cloned.1.call-update) | async-done | bytes 1572880 | tf_op jit(solution)/shard_map/all_gather | solution.py:79
  137.7 2.6 fusion.48
  140.3 75.2 %while.13 = (s32[]{:T(128)}, f32[3072,256]{0,1:T(8,128)S(1)}, bf16[8,192,128]{2,1,0:T(8,128)(2,1)}, bf16[8,192,128]{2,1,0:T(8,128)(2,1)}, bf16[3072,128]{1,0:T(8...) while((s32[]{:T(128)}, f32[3072,256]{0,1:T(8,128)S(1)}, ...), condition=%wide.region_9.10_spmd.clone, body=%wide.region_5.9_spmd.clone.sunk | while | flops 922410432 | bytes 42505748 | solution.py:57
  140.3 1.9 fusion.87
  146.3 1.1 fusion.93
  147.4 1.2 convolution_multiply_fusion.5
  149.7 1.9 fusion.87
  156.8 1.2 convolution_multiply_fusion.5
  159.1 1.9 fusion.87
  166.2 1.2 convolution_multiply_fusion.5
  168.5 1.9 fusion.87
  175.6 1.2 convolution_multiply_fusion.5
  177.9 1.9 fusion.87
  185.0 1.2 convolution_multiply_fusion.5
  187.3 1.9 fusion.87
  194.4 1.2 convolution_multiply_fusion.5
  196.7 1.9 fusion.87
  203.8 1.2 convolution_multiply_fusion.5
  206.1 1.9 fusion.87
  213.2 1.2 convolution_multiply_fusion.5
  215.5 1.4 convert_element_type.40
  216.8 2.6 copy.28
  219.5 53.6 %reduce-scatter.7.cloned.1.call-done = bf16[192,256]{1,0:T(8,128)(2,1)} async-done(((bf16[3072,256]{1,0:T(8,128)(2,1)}), bf16[192,256]{1,0:T(8,128)(2,1)}) %reduce-scatter.7.cloned.1.call-update) | async-done | bytes 98320
  273.1 8.4 %fusion.26 = bf16[16384,256]{0,1:T(8,128)(2,1)} fusion(bf16[192,256]{1,0:T(8,128)(2,1)} %reduce-scatter.7.cloned.1.call-done, bf16[1,192,16384]{2,1,0:T(8,128)(2,1)} %param.9), kind=kOutput, calls=%fused_computation.34 | convolution fusion | flops 1614807040 | bytes 14778368 | tf_op jit(solution)/shard_map/dot_general | solution.py:102
  281.7 90.6 %reduce-scatter.5.cloned.1.call-done = bf16[1024,256]{0,1:T(8,128)(2,1)} async-done(((bf16[16384,256]{0,1:T(8,128)(2,1)}), bf16[1024,256]{0,1:T(8,128)(2,1)}) %reduce-scatter.5.cloned.1.call-update) | async-done | bytes 524304 | tf_op jit(solution)/shard_map/reduce_scatter | solution.py:101
  373.5 111.3 %all-reduce.2.cloned.1.call-done = bf16[1024,256]{0,1:T(8,128)(2,1)} async-done(((bf16[1024,256]{0,1:T(8,128)(2,1)}), bf16[1024,256]{0,1:T(8,128)(2,1)}) %all-reduce.2.cloned.1.call-update) | async-done | bytes 524304 | tf_op jit(solution)/shard_map/psum | solution.py:109
  484.9 1.1 fusion.49
  (154 shorter events, 55.6 us)
Async XLA Ops:
  7.2 83.4 %all-gather.3.cloned.1.call-start = ((), (), s32[]{:S(2)}) async-start(), calls=%async_computation.2 | async-start | bytes 8912896 | tf_op jit(solution)/shard_map/all_gather | solution.py:76
  9.1 89.2 %copy-start.7 = (s32[1,8]{1,0:T(1,128)S(1)}, s32[1,8]{1,0:T(1,128)}, u32[]{:S(2)}) copy-start(s32[1,8]{1,0:T(1,128)} %param.15) | copy-start | bytes 100
  9.1 89.9 %copy-start.3 = (bf16[1,192,1024]{2,1,0:T(8,128)(2,1)S(1)}, bf16[1,192,1024]{2,1,0:T(8,128)(2,1)}, u32[]{:S(2)}) copy-start(bf16[1,192,1024]{2,1,0:T(8,128)(2,1)} %param.10) | copy-start | bytes 1179652
  9.1 128.6 %all-gather.5.cloned.1.call-start = ((), (), s32[]{:S(2)}) async-start(), calls=%async_computation.3 | async-start | bytes 1671168 | tf_op jit(solution)/shard_map/all_gather | solution.py:79
  98.2 2.9 copy-start.6
  98.3 174.9 %reduce-scatter.7.cloned.1.call-start = ((), (), s32[]{:S(2)}) async-start(), calls=%async_computation.6 | async-start | bytes 1671168
  140.3 1.9 copy-start.2
  140.3 1.9 copy-start.5
  143.0 1.1 copy-start
  149.7 1.9 copy-start.2
  149.7 1.9 copy-start.5
  152.4 1.1 copy-start
  159.1 1.9 copy-start.2
  159.1 1.9 copy-start.5
  161.8 1.1 copy-start
  168.5 1.9 copy-start.2
  168.5 1.9 copy-start.5
  171.2 1.1 copy-start
  177.9 1.9 copy-start.2
  177.9 1.9 copy-start.5
  180.6 1.1 copy-start
  187.3 1.9 copy-start.2
  187.3 1.9 copy-start.5
  190.0 1.1 copy-start
  196.7 1.9 copy-start.2
  196.7 1.9 copy-start.5
  199.4 1.1 copy-start
  206.1 1.9 copy-start.2
  206.1 1.9 copy-start.5
  219.5 152.8 %reduce-scatter.5.cloned.1.call-start = ((), (), s32[]{:S(2)}) async-start(), calls=%async_computation.4 | async-start | bytes 8912896 | tf_op jit(solution)/shard_map/reduce_scatter | solution.py:101
  281.6 90.7 %copy-start.4 = (bf16[8,192,128]{2,1,0:T(8,128)(2,1)S(1)}, bf16[8,192,128]{2,1,0:T(8,128)(2,1)}, u32[]{:S(2)}) copy-start(bf16[8,192,128]{2,1,0:T(8,128)(2,1)} %get-tuple-element.46) | copy-start | bytes 1179652
  281.6 203.2 %all-reduce.2.cloned.1.call-start = ((), (), s32[]{:S(2)}) async-start(), calls=%async_computation.5 | async-start | bytes 1048576 | tf_op jit(solution)/shard_map/psum | solution.py:109
  (9 other events, 10.2 us)
Sparse Core Ops, SparseCore 0:
  11.0 79.5 all-gather.2
  98.4 39.2 all-gather.4
  219.6 53.5 reduce-scatter.6
  281.7 90.5 reduce-scatter.4
  374.6 110.2 all-reduce.1
where the time goes:
time: 496 us; the launch traced here: 495 us
  waiting for transfers between devices  370 us (75%)
  matrix products  61.1 us (12%)
  other arithmetic  28.8 us (6%)
  local copies, waits for them, and re-layouts  19.4 us (4%)
  between operations  13.9 us (3%)
    psum x1, waiting for transfers between devices, on_device(): weight_grads = lax.psum(partial_rows, 'ctx').astype(jnp.float32)  111 us
    reduce_scatter x1, waiting for transfers between devices, on_device(): lax.psum_scatter(lax.dot_general(columns, kv_grads, (((0,), (0,)), ((), (...  90.6 us
    all_gather x1, waiting for transfers between devices, on_device(): lax.all_gather(stacked, 'dp', axis=0, tiled=True)  81.4 us
    unnamed x6, waiting for transfers between devices  53.7 us
    all_gather x1, waiting for transfers between devices, on_device(): gathered = lax.all_gather(projected, 'ctx', axis=0, tiled=True)  33.1 us
    dot_general x8, matrix products, one_head(): jnp.dot(query_one, jnp.transpose(key_rows), preferred_element_type=jnp.fl...  15 us
  transfers between devices with their start and end apart: 5, of which 5 were waited for; matrix products, arithmetic and copies ran while one was open for 1% of the time, Pallas kernels for 0%

commit v1 on v0

--- a/solution.py
+++ b/solution.py
@@ -3,6 +3,13 @@
 import jax.numpy as jnp
 from jax import lax
 from jax.sharding import PartitionSpec as P
+
+run_mix = lambda panel, named_axis: jnp.concatenate(
+    lax.all_to_all(
+        jnp.stack([panel for _ in range(lax.axis_size(named_axis))], axis=0), named_axis, 0, 0
+    ),
+    0,
+)
 
 
 def table_lookup(slots, table):
@@ -71,11 +78,9 @@
     seq_rows = row_count * ctx_count
     stacked = jnp.concatenate([w_key, w_value], axis=1)
     columns = inputs
-    projected = jnp.dot(
-        columns,
-        lax.all_gather(stacked, "dp", axis=0, tiled=True),
-        preferred_element_type=jnp.float32,
-    ).astype(jnp.bfloat16)
+    projected = jnp.dot(columns, run_mix(stacked, "dp"), preferred_element_type=jnp.float32).astype(
+        jnp.bfloat16
+    )
     gathered = lax.all_gather(projected, "ctx", axis=0, tiled=True)
     doc_ends = jnp.cumsum(doc_lengths[0])
     every_row = jnp.arange(seq_rows, dtype=jnp.int32)

time: 496 us -> 582 us (1.17)
  blocking collectives: 0 us -> 102 us
  waiting for transfers between devices: 370 us -> 291 us
  other arithmetic: 28.8 us -> 65.4 us
  matrix products: 61.1 us -> 93.6 us
  local copies, waits for them, and re-layouts: 19.4 us -> 11.8 us
    all_to_all x0 -> x1, blocking collectives: none -> 102 us  [lax.all_to_all(jnp.stack([panel for _ in range(lax.axis_size(named_axis))...]
    all_gather x1 -> x0, waiting for transfers between devices: 81.4 us -> none  [on_device(): lax.all_gather(stacked, 'dp', axis=0, tiled=True)]
    add x8, other arithmetic: 8.47 us -> 35.8 us  [one_head(): running + jnp.concatenate([key_grad, value_grad], axis=1)]
    dot_general x8, matrix products: 3.42 us -> 18.9 us  [one_head(): lax.dot_general(probs_low, cot_one, (((0,), (0,)), ((), ())), preferred_e...]
    dot_general x8, matrix products: 8.62 us -> 17.7 us  [one_head(): jnp.dot(dscore, key_rows, preferred_element_type=jnp.float32) * score_scale]
    while x64 -> x0, local copies, waits for them, and re-layouts: 7.9 us -> none
    dot_general x8, matrix products: 4.4 us -> 10.9 us  [one_head(): jnp.dot(probs_low, value_rows, preferred_element_type=jnp.float32)]
    dot_general x8, matrix products: 3.88 us -> 10.2 us  [one_head(): jnp.dot(cot_one, jnp.transpose(value_rows), preferred_element_type=jnp.fl...]
  transfers between devices with their start and end apart: 5 -> 4, of which waited for: 5 -> 4; matrix products, arithmetic and copies ran while one was open for 1% -> 1% of each run, Pallas kernels for 0% -> 0%
where the time goes in v1:
time: 582 us; the launch traced here: 579 us
  waiting for transfers between devices  291 us (50%)
  blocking collectives  102 us (18%)
  matrix products  93.6 us (16%)
  other arithmetic  65.4 us (11%)
  between operations  13.9 us (2%)
  local copies, waits for them, and re-layouts  11.8 us (2%)
    psum x1, waiting for transfers between devices, on_device(): weight_grads = lax.psum(partial_rows, 'ctx').astype(jnp.float32)  110 us
    all_to_all x1, blocking collectives, lax.all_to_all(jnp.stack([panel for _ in range(lax.axis_size(named_axis))...  102 us
    reduce_scatter x1, waiting for transfers between devices, on_device(): lax.psum_scatter(lax.dot_general(columns, kv_grads, (((0,), (0,)), ((), (...  90.8 us
    unnamed x5, waiting for transfers between devices  53.7 us
    all_gather x1, waiting for transfers between devices, on_device(): gathered = lax.all_gather(projected, 'ctx', axis=0, tiled=True)  36.4 us
    add x8, other arithmetic, one_head(): running + jnp.concatenate([key_grad, value_grad], axis=1)  35.8 us
    dot_general x8, matrix products, one_head(): lax.dot_general(probs_low, cot_one, (((0,), (0,)), ((), ())), preferred_e...  18.9 us
    dot_general x8, matrix products, one_head(): jnp.dot(dscore, key_rows, preferred_element_type=jnp.float32) * score_scale  17.7 us
  transfers between devices with their start and end apart: 4, of which 4 were waited for; matrix products, arithmetic and copies ran while one was open for 1% of the time, Pallas kernels for 0%

profile of v1, /device:TPU:1, one launch (start us, length us, event | category | flops | bytes accessed | tf_op | source)
XLA Modules:
  0.0 578.7 jit_solution(14378515027988148759)
XLA Ops:
  9.1 102.4 %all_to_all.5 = bf16[16,1024,256]{2,1,0:T(8,128)(2,1)S(1)} all-to-all(bf16[16,1024,256]{2,1,0:T(8,128)(2,1)S(1)} %stack.2), channel_id=1, replica_groups=mesh['dp'=16,'ctx'=16] {'dp'}, dimensions={0} | all-to-all | bytes 16777216 | tf_op jit(solution)/shard_map/all_to_all | solution.py:8
  111.6 2.7 fusion.33
  118.0 36.4 %all-gather.2.cloned.1.call-done = bf16[3072,256]{1,0:T(8,128)(2,1)} async-done(((bf16[192,256]{1,0:T(8,128)(2,1)}), bf16[3072,256]{1,0:T(8,128)(2,1)}) %all-gather.2.cloned.1.call-update) | async-done | bytes 1572880 | tf_op jit(solution)/shard_map/all_gather | solution.py:84
  154.4 2.4 fusion.48
  156.8 143.1 %while.13 = (s32[]{:T(128)}, f32[3072,256]{0,1:T(8,128)}, bf16[8,192,128]{2,1,0:T(8,128)(2,1)}, bf16[8,192,128]{2,1,0:T(8,128)(2,1)}, bf16[3072,128]{1,0:T(8,128...) while((s32[]{:T(128)}, f32[3072,256]{0,1:T(8,128)}, ...), condition=%wide.region_9.10_spmd.clone, body=%wide.region_5.9_spmd.clone.sunk | while | flops 922410432 | bytes 36164232 | solution.py:64
  165.6 2.4 fusion.90
  168.0 3.6 maximum_add_fusion.2
  171.6 2.2 fusion.93
  182.6 2.4 fusion.90
  185.0 4.6 maximum_add_fusion.2
  189.6 2.2 fusion.93
  200.7 2.4 fusion.90
  203.0 4.6 maximum_add_fusion.2
  207.6 2.2 fusion.93
  218.7 2.4 fusion.90
  221.0 4.6 maximum_add_fusion.2
  225.6 2.2 fusion.93
  236.7 2.4 fusion.90
  239.0 4.6 maximum_add_fusion.2
  243.6 2.2 fusion.93
  254.7 2.4 fusion.90
  257.0 4.6 maximum_add_fusion.2
  261.6 2.2 fusion.93
  272.7 2.4 fusion.90
  275.0 4.6 maximum_add_fusion.2
  279.6 2.2 fusion.93
  290.7 2.4 fusion.90
  293.0 4.6 maximum_add_fusion.2
  303.6 53.6 %reduce-scatter.7.cloned.1.call-done = bf16[192,256]{1,0:T(8,128)(2,1)} async-done(((bf16[3072,256]{1,0:T(8,128)(2,1)}), bf16[192,256]{1,0:T(8,128)(2,1)}) %reduce-scatter.7.cloned.1.call-update) | async-done | bytes 98320
  357.2 8.4 %fusion.26 = bf16[16384,256]{0,1:T(8,128)(2,1)} fusion(bf16[192,256]{1,0:T(8,128)(2,1)} %reduce-scatter.7.cloned.1.call-done, bf16[1,192,16384]{2,1,0:T(8,128)(2,1)} %param.9), kind=kOutput, calls=%fused_computation.34 | convolution fusion | flops 1614807040 | bytes 14778368 | tf_op jit(solution)/shard_map/dot_general | solution.py:107
  365.8 90.8 %reduce-scatter.5.cloned.1.call-done = bf16[1024,256]{0,1:T(8,128)(2,1)} async-done(((bf16[16384,256]{0,1:T(8,128)(2,1)}), bf16[1024,256]{0,1:T(8,128)(2,1)}) %reduce-scatter.5.cloned.1.call-update) | async-done | bytes 524304 | tf_op jit(solution)/shard_map/reduce_scatter | solution.py:106
  458.8 110.2 %all-reduce.2.cloned.1.call-done = bf16[1024,256]{0,1:T(8,128)(2,1)} async-done(((bf16[1024,256]{0,1:T(8,128)(2,1)}), bf16[1024,256]{0,1:T(8,128)(2,1)}) %all-reduce.2.cloned.1.call-update) | async-done | bytes 524304 | tf_op jit(solution)/shard_map/psum | solution.py:114
  (94 shorter events, 87.3 us)
Async XLA Ops:
  7.2 147.2 %all-gather.2.cloned.1.call-start = ((), (), s32[]{:S(2)}) async-start(), calls=%async_computation.3 | async-start | bytes 1671168 | tf_op jit(solution)/shard_map/all_gather | solution.py:84
  8.3 103.3 %slice-start = ((s8[6291456]{0:T(1024)(128)(4,1)}), s8[2097152]{0:T(1024)(128)(4,1)S(1)}, s32[]{:S(2)}) async-start(s8[6291456]{0:T(1024)(128)(4,1)} %bitcast.78), calls=%async_computation.7 | async-start | bytes 4194304
  9.1 102.4 %slice-start.1 = ((s8[6291456]{0:T(1024)(128)(4,1)}), s8[4194304]{0:T(1024)(128)(4,1)S(1)}, s32[]{:S(2)}) async-start(s8[6291456]{0:T(1024)(128)(4,1)} %bitcast.78), calls=%async_computation.8 | async-start | bytes 8388608
  111.6 2.8 copy-start.3
  111.6 3.0 copy-start
  111.6 3.9 copy-start.1
  114.3 2.1 copy-start.2
  114.3 243.0 %reduce-scatter.7.cloned.1.call-start = ((), (), s32[]{:S(2)}) async-start(), calls=%async_computation.6 | async-start | bytes 1671168
  303.6 153.0 %reduce-scatter.5.cloned.1.call-start = ((), (), s32[]{:S(2)}) async-start(), calls=%async_computation.4 | async-start | bytes 8912896 | tf_op jit(solution)/shard_map/reduce_scatter | solution.py:106
  365.7 203.3 %all-reduce.2.cloned.1.call-start = ((), (), s32[]{:S(2)}) async-start(), calls=%async_computation.5 | async-start | bytes 1048576 | tf_op jit(solution)/shard_map/psum | solution.py:114
Sparse Core Ops, SparseCore 0:
  114.4 39.9 all-gather.1
  303.7 53.5 reduce-scatter.6
  365.8 90.6 reduce-scatter.4
  458.8 110.1 all-reduce.1
